TPU v7x, 256 devices: a whole 4x4x8 slice. The times are simulated.
256 devices in a mesh: dp: 16 (over x, y), tensor: 16 (over z, core).
Axes of the slice: x: 4, y: 4, z: 8, core: 2. Of those that a mesh axis runs over, the one named last changes fastest.
Arguments:
- tokens: bfloat16 [8192, 7424], P(('dp', 'tensor')), may hold values from -6 to 6
- out_grad: bfloat16 [8192, 7424], P(('dp', 'tensor')), may hold values from -6 to 6
- gate_pre: bfloat16 [8192, 29696], P('dp', 'tensor'), may hold values from -8 to 8
- up_pre: bfloat16 [8192, 29696], P('dp', 'tensor'), may hold values from -6 to 6
- hidden_grad: bfloat16 [8192, 29696], P('dp', 'tensor'), may hold values from -6 to 6
- warm_basis: bfloat16 [3, 64, 29696], P(None, None, 'tensor'), may hold values from -0.03125 to 0.03125
Outputs:
- factor_left: float32 [3, 64, 7424], P(None, None, 'tensor')
- factor_right: float32 [3, 64, 29696], P(None, None, 'tensor')
All inputs are finite; a program needn't handle non-finite values.
Results may differ from a plain program's by a relative error of at most 0.0048.
Values may be sent and summed in bfloat16 or wider, within the bound.
A program may use at most 128 MiB of HBM per device.

v0:
```python
import jax
import jax.numpy as jnp
from jax import lax
from jax.sharding import PartitionSpec as P


def swiglu_stack(gate_pre, up_pre, hidden_grad):
    gate_value = gate_pre.astype(jnp.float32)
    up_value = up_pre.astype(jnp.float32)
    grad_value = hidden_grad.astype(jnp.float32)
    sigmoid_value = jax.nn.sigmoid(gate_value)
    silu_value = gate_value * sigmoid_value
    silu_slope = sigmoid_value * (1.0 + gate_value * (1.0 - sigmoid_value))
    hidden = (silu_value * up_value).astype(jnp.bfloat16)
    gate_grad = (grad_value * up_value * silu_slope).astype(jnp.bfloat16)
    up_grad = (grad_value * silu_value).astype(jnp.bfloat16)
    return jnp.stack([gate_grad, up_grad, hidden])


def orthonormal(left_sum, gram_matrix):
    lower_factor = jnp.linalg.cholesky(gram_matrix)
    return lax.linalg.triangular_solve(lower_factor, left_sum, left_side=True, lower=True)


def gram_of(left_sum):
    return jnp.einsum("krd,ksd->krs", left_sum, left_sum, precision=lax.Precision.HIGHEST)


def shards(tokens, out_grad, gate_pre, up_pre, hidden_grad, warm_basis):
    highest = lax.Precision.HIGHEST
    right_side = swiglu_stack(gate_pre, up_pre, hidden_grad)
    kinds = warm_basis.shape[0]
    rank_size = warm_basis.shape[1]
    local_rows = tokens.shape[0]
    rows = right_side
    term = jnp.einsum("ktf,krf->tkr", rows, warm_basis, preferred_element_type=jnp.float32)
    coeff = lax.psum_scatter(
        term.reshape(lax.axis_size("tensor") * local_rows, kinds * rank_size),
        "tensor",
        scatter_dimension=0,
        tiled=True,
    )
    coeff = coeff.reshape(local_rows, kinds, rank_size)
    width_part = tokens.shape[1] // lax.axis_size("tensor")
    left_side = jnp.stack([tokens, tokens, out_grad]).astype(jnp.float32)
    partial_left = jnp.einsum("tkr,ktd->krd", coeff, left_side, precision=highest)
    left_sum = lax.psum(partial_left, ("dp", "tensor"))
    factor_full = orthonormal(left_sum, gram_of(left_sum))
    own_cols = lax.dynamic_slice_in_dim(
        factor_full, lax.axis_index("tensor") * width_part, width_part, 2
    )
    proj = jnp.einsum("krd,ktd->krt", factor_full, left_side, precision=highest).astype(
        jnp.bfloat16
    )
    rows = right_side
    right_terms = jnp.einsum(
        "krt,ktf->krf",
        lax.all_gather(proj, "tensor", axis=2, tiled=True),
        rows,
        preferred_element_type=jnp.float32,
    )
    factor_right = lax.psum(right_terms, "dp") / lax.axis_size("dp")
    return (own_cols, factor_right)


def solution(mesh):
    placed = (
        P(("dp", "tensor"), None),
        P(("dp", "tensor"), None),
        P("dp", "tensor"),
        P("dp", "tensor"),
        P("dp", "tensor"),
        P(None, None, "tensor"),
    )
    return jax.shard_map(
        shards,
        mesh=mesh,
        in_specs=placed,
        out_specs=(P(None, None, "tensor"), P(None, None, "tensor")),
        check_vma=False,
    )
```

profile of v0, /device:TPU:8, one launch (start us, length us, event | category | flops | bytes accessed | tf_op | source)
XLA Modules:
  0.0 531.9 jit_solution(17496836282244683737)
XLA Ops:
  7.2 0.0 copy-start
  7.2 0.0 reduce-scatter.2.cloned.1.call-start
  7.2 4.2 fusion.13
  11.5 0.0 copy-start.6
  11.5 1.2 fusion.10
  12.7 0.1 copy-done.2
  12.8 0.6 copy-done.4
  13.4 1.0 copy.14
  14.4 0.0 reduce-scatter.2.cloned.1.call-update
  14.4 0.0 all-reduce.3.cloned.1.call-start
  14.4 59.5 %reduce-scatter.2.cloned.1.call-done = f32[32,192]{1,0:T(8,128)} async-done(((f32[512,192]{1,0:T(8,128)}), f32[32,192]{1,0:T(8,128)}) %reduce-scatter.2.cloned.1.call-update) | async-done | bytes 24592 | tf_op jit(solution)/shard_map/reduce_scatter | solution.py:37
  74.0 0.8 reshape.21
  74.8 6.1 %fusion.14 = f32[3,64,7424]{2,1,0:T(8,128)} fusion(bf16[1,32,7424]{2,1,0:T(8,128)(2,1)S(1)} %bitcast.26, bf16[1,32,7424]{2,1,0:T(8,128)(2,1)} %bitcast.28, f32[32,3,64]{2,1,0:T(4,128)S(1)} %reshape.21), kind=kOutput, calls=%fused_computation.23 | convolution fusion | flops 548782080 | bytes 6676480 | tf_op jit(solution)/shard_map/tkr,ktd->krd/dot_general | solution.py:46
  81.0 0.0 all-reduce.3.cloned.1.call-update
  81.0 0.0 all-reduce.5.cloned.1.call-start
  81.1 271.4 %all-reduce.3.cloned.1.call-done = f32[3,64,7424]{2,1,0:T(8,128)} async-done(((f32[3,64,7424]{2,1,0:T(8,128)}), f32[3,64,7424]{2,1,0:T(8,128)}) %all-reduce.3.cloned.1.call-update) | async-done | bytes 5701648 | tf_op jit(solution)/shard_map/psum | solution.py:47
  352.5 9.5 %fusion.23 = f32[3,64,64]{2,1,0:T(8,128)S(1)} fusion(f32[3,64,7424]{2,1,0:T(8,128)} %all-reduce.3.cloned.1.call-done), kind=kOutput, calls=%fused_computation.40 | convolution fusion | flops 1094713344 | bytes 5750784 | tf_op jit(solution)/shard_map/krd,ksd->krs/dot_general | solution.py:26
  362.0 0.1 copy.16
  362.1 17.8 %custom-call.7 = f32[3,64,64]{2,1,0:T(8,128)S(1)} custom-call(f32[3,64,64]{2,1,0:T(8,128)S(1)} %fusion.17), custom_call_target="Cholesky" | custom-call | tf_op jit(solution)/shard_map/jit(cholesky)/cholesky | solution.py:21
  379.9 0.1 compare_reduce_fusion
  380.0 0.1 select_bitcast_fusion
  380.1 14.7 %custom-call.8 = f32[3,1,64,64]{2,3,1,0:T(8,128)S(1)} custom-call(f32[3,1,64,64]{3,2,1,0:T(8,128)S(1)} %select_bitcast_fusion), custom_call_target="InvertDiagBlocksLowerTriangular" | custom-call | tf_op jit(solution)/shard_map/triangular_solve | solution.py:22
  394.9 0.0 copy-start.7
  394.9 7.1 %fusion.15 = f32[3,64,7424]{2,1,0:T(8,128)S(1)} fusion(f32[3,64,7424]{2,1,0:T(8,128)} %all-reduce.3.cloned.1.call-done, f32[3,1,64,64]{2,3,1,0:T(8,128)S(1)} %custom-call.8), kind=kOutput, calls=%fused_computation.25 | convolution fusion | flops 1094713344 | bytes 11452416 | tf_op jit(solution)/shard_map/triangular_solve | solution.py:22
  402.0 2.4 copy-done.1
  404.5 2.8 convolution_convert_fusion
  407.3 15.5 %all_gather.3 = bf16[3,64,512]{1,2,0:T(8,128)(2,1)S(1)} all-gather(bf16[3,64,32]{1,2,0:T(8,128)(2,1)S(1)} %convolution_convert_fusion), channel_id=1, replica_groups=mesh['dp'=16,'tensor'=16] {'tensor'}, dimensions={2}, use_global_device_ids=true | all-gather | bytes 208896 | tf_op jit(solution)/shard_map/all_gather | solution.py:58
  422.8 2.9 fusion.9
  425.7 0.0 all-reduce.5.cloned.1.call-update
  425.7 2.0 constant_dynamic-slice_fusion
  427.7 95.1 %all-reduce.5.cloned.1.call-done = f32[3,64,1856]{2,1,0:T(8,128)} async-done(((f32[3,64,1856]{2,1,0:T(8,128)}), f32[3,64,1856]{2,1,0:T(8,128)}) %all-reduce.5.cloned.1.call-update) | async-done | bytes 1425424 | tf_op jit(solution)/shard_map/psum | solution.py:62
  522.8 2.6 broadcast_multiply_fusion
  (14 shorter events, 0.1 us)
Async XLA Ops:
  7.2 4.3 copy-start
  7.2 66.8 %reduce-scatter.2.cloned.1.call-start = ((), (), s32[]{:S(2)}) async-start(), calls=%async_computation.1 | async-start | bytes 557056 | tf_op jit(solution)/shard_map/reduce_scatter | solution.py:37
  11.5 1.3 copy-start.2
  11.5 1.9 copy-start.4
  11.5 63.3 %copy-start.6 = (bf16[32,7424]{1,0:T(8,128)(2,1)S(1)}, bf16[32,7424]{1,0:T(8,128)(2,1)}, u32[]{:S(2)}) copy-start(bf16[32,7424]{1,0:T(8,128)(2,1)} %param.7) | copy-start | bytes 1425412
  14.4 338.1 %all-reduce.3.cloned.1.call-start = ((), (), s32[]{:S(2)}) async-start(), calls=%async_computation.2 | async-start | bytes 11403264 | tf_op jit(solution)/shard_map/psum | solution.py:47
  81.0 441.8 %all-reduce.5.cloned.1.call-start = ((), (), s32[]{:S(2)}) async-start(), calls=%async_computation.3 | async-start | bytes 2949120 | tf_op jit(solution)/shard_map/psum | solution.py:62
  394.9 9.6 %copy-start.7 = (bf16[32,7424]{1,0:T(8,128)(2,1)S(1)}, bf16[32,7424]{1,0:T(8,128)(2,1)}, u32[]{:S(2)}) copy-start(bf16[32,7424]{1,0:T(8,128)(2,1)} %param.6) | copy-start | bytes 1425412
  402.0 2.5 copy-start.1
  404.4 18.3 %copy-start.3 = (bf16[1,512,1856]{1,2,0:T(8,128)(2,1)S(1)}, bf16[1,512,1856]{1,2,0:T(8,128)(2,1)}, u32[]{:S(2)}) copy-start(bf16[1,512,1856]{1,2,0:T(8,128)(2,1)} %copy-done.2) | copy-start | bytes 5701636
  404.4 18.3 %copy-start.5 = (bf16[1,512,1856]{1,2,0:T(8,128)(2,1)S(1)}, bf16[1,512,1856]{1,2,0:T(8,128)(2,1)}, u32[]{:S(2)}) copy-start(bf16[1,512,1856]{1,2,0:T(8,128)(2,1)} %copy-done.4) | copy-start | bytes 5701636
Sparse Core Ops, SparseCore 0:
  14.5 59.4 reduce-scatter.1
  81.1 271.3 all-reduce.2
  425.8 96.9 all-reduce.4
where the time goes:
time: 532 us
  waiting for transfers between devices  426 us (80%)
  other arithmetic  39.6 us (7%)
  matrix products  29.6 us (6%)
  blocking collectives  15.5 us (3%)
  between operations  13.9 us (3%)
  local copies, waits for them, and re-layouts  7.05 us (1%)
    psum x1, waiting for transfers between devices, shards(): left_sum = lax.psum(partial_left, ('dp', 'tensor'))  271 us
    psum x1, waiting for transfers between devices, shards(): factor_right = lax.psum(right_terms, 'dp') / lax.axis_size('dp')  95.1 us
    reduce_scatter x1, waiting for transfers between devices, shards(): lax.psum_scatter(term.reshape(lax.axis_size('tensor') * local_rows, kinds...  59.5 us
    another operation x4, other arithmetic, orthonormal(): lower_factor = jnp.linalg.cholesky(gram_matrix)  17.9 us
    all_gather x1, blocking collectives, shards(): lax.all_gather(proj, 'tensor', axis=2, tiled=True)  15.5 us
    another operation x3, other arithmetic, orthonormal(): lax.linalg.triangular_solve(lower_factor, left_sum, left_side=True, lower...  14.8 us
  transfers between devices with their start and end apart: 3, of which 3 were waited for; matrix products, arithmetic and copies ran while one was open for 0% of the time, Pallas kernels for 0%

commit v1 on v0

v1 whole, which is shorter than its diff:
```python
import functools

import jax
import jax.numpy as jnp
from jax import lax
from jax.experimental import pallas as pl
from jax.experimental.pallas import tpu as pltpu
from jax.sharding import PartitionSpec as P

MESH = pl.DeviceIdType.MESH
F32 = jnp.float32
BF16 = jnp.bfloat16
HIGHEST = lax.Precision.HIGHEST

ROWS = 32
DW = 464
DWP = 512
FFW = 1856
GROUP = 512
CHUNK = 128
NCHUNK = GROUP // CHUNK
LANE_BLOCKS = ((0, 512), (512, 512), (1024, 512), (1536, 320))


def dot(a, b, dims, precision=None):
    return lax.dot_general(a, b, (dims, ((), ())), precision=precision, preferred_element_type=F32)


NN = ((1,), (0,))
NT = ((1,), (1,))


def split(value):
    high = value.astype(BF16)
    return high, (value - high.astype(F32)).astype(BF16)


def kernel(
    tok_hbm, og_hbm, gate_hbm, up_hbm, hid_hbm, warm_hbm,
    out_left, out_right,
    tok, og, gate, up, hid, wp,
    apad, arecv, bmat, cpart, csib, csum, crecv, cgath,
    lpart, lsib, lsum, lrecv, lfull,
    upart, urecv, gpart, grecv, gfull,
    pown, pgath, lown, lout,
    rpart, rrecv, rown, rgath,
    ldma, cdma, ssem, rsem,
):
    dp = lax.axis_index("dp")
    t = lax.axis_index("tensor")
    x, y = dp // 4, dp % 4
    z, c = t // 2, t % 2

    def d_peer(d):
        return ((x + d // 4) % 4) * 4 + (y + d % 4) % 4

    def d_back(d):
        return ((x + 4 - d // 4) % 4) * 4 + (y + 4 - d % 4) % 4

    def z_peer(d):
        return (z + d) % 8

    def remote(src, dst, i, device):
        return pltpu.make_async_remote_copy(
            src, dst, ssem.at[i], rsem.at[i], device_id=device, device_id_type=MESH
        )

    def arrived(ref, i):
        pltpu.make_async_copy(ref, ref, rsem.at[i]).wait()

    def sent(ref, i):
        pltpu.make_async_copy(ref, ref, ssem.at[i]).wait()

    def each(n, body):
        def step(i, carry):
            body(i)
            return carry
        lax.fori_loop(1, n, step, 0)

    barrier = pltpu.get_barrier_semaphore()
    each(16, lambda d: pl.semaphore_signal(barrier, inc=1, device_id=(d_peer(d), t), device_id_type=MESH))
    each(16, lambda d: pl.semaphore_signal(barrier, inc=1, device_id=(dp, (t + d) % 16), device_id_type=MESH))

    copies = [
        pltpu.make_async_copy(tok_hbm, tok, ldma.at[0]),
        pltpu.make_async_copy(og_hbm, og, ldma.at[1]),
        pltpu.make_async_copy(warm_hbm.at[0], wp.at[0, pl.ds(0, 64)], ldma.at[2]),
        pltpu.make_async_copy(warm_hbm.at[1], wp.at[1, pl.ds(64, 64)], ldma.at[3]),
        pltpu.make_async_copy(warm_hbm.at[2], wp.at[2, pl.ds(0, 64)], ldma.at[4]),
        pltpu.make_async_copy(warm_hbm.at[2], wp.at[2, pl.ds(64, 64)], ldma.at[5]),
    ]
    for copy in copies:
        copy.start()
    chunk_copies = []
    for ch in range(NCHUNK):
        rows = pl.ds(ch * CHUNK, CHUNK)
        group = [
            pltpu.make_async_copy(src.at[rows], dst.at[rows], cdma.at[i, ch])
            for i, (src, dst) in enumerate(((gate_hbm, gate), (up_hbm, up), (hid_hbm, hid)))
        ]
        for copy in group:
            copy.start()
        chunk_copies.append(group)
    wp[0, 64:128, :] = jnp.zeros((64, FFW), BF16)
    wp[1, 0:64, :] = jnp.zeros((64, FFW), BF16)

    copies[0].wait()
    copies[1].wait()
    keep = lax.broadcasted_iota(jnp.int32, (ROWS, DWP), 1) < DW
    for which, ref in enumerate((tok, og)):
        for g in range(16):
            first = (DW * g) // 128
            shift = DW * g - 128 * first
            width = 512 if shift <= 48 else 640
            wide = ref[:, 128 * first : 128 * first + width].astype(F32)
            if shift:
                wide = pltpu.roll(wide, width - shift, 1)
            apad[which, g] = jnp.where(keep, wide[:, :DWP], 0.0).astype(BF16)
    for copy in copies[2:]:
        copy.wait()

    lane = lax.broadcasted_iota(jnp.int32, (16, 128), 1)
    for ch in range(NCHUNK):
        if ch == 2:
            pl.semaphore_wait(barrier, 30)

            def scatter_tokens(d):
                for which in range(2):
                    remote(apad.at[which, d_peer(d)], arecv.at[which, d], which, (d_peer(d), t)).start()

            each(16, scatter_tokens)
        for copy in chunk_copies[ch]:
            copy.wait()

        def swiglu(i, carry):
            rows = pl.ds(pl.multiple_of(ch * CHUNK + i * 16, 16), 16)
            for start, width in LANE_BLOCKS:
                cols = pl.ds(start, width)
                g = gate[rows, cols].astype(F32)
                u = up[rows, cols].astype(F32)
                h = hid[rows, cols].astype(F32)
                s = 0.5 * jnp.tanh(0.5 * g) + 0.5
                silu = g * s
                slope = s * (1.0 + g * (1.0 - s))
                bmat[0, rows, cols] = (h * u * slope).astype(BF16)
                bmat[1, rows, cols] = (h * silu).astype(BF16)
                bmat[2, rows, cols] = (silu * u).astype(BF16)
            return carry

        lax.fori_loop(0, CHUNK // 16, swiglu, 0)
        rows = pl.ds(ch * CHUNK, CHUNK)
        c01 = dot(bmat[0, rows, :], wp[0], NT) + dot(bmat[1, rows, :], wp[1], NT)
        c22 = dot(bmat[2, rows, :], wp[2], NT)
        for i in range(CHUNK // ROWS):
            owner = ch * (CHUNK // ROWS) + i
            cpart[owner % 2, owner // 2, 0:32, :] = c01[32 * i : 32 * i + 32]
            cpart[owner % 2, owner // 2, 32:48, :] = jnp.where(
                lane < 64, c22[32 * i : 32 * i + 16], c22[32 * i + 16 : 32 * i + 32]
            )

    sibling = (dp, 2 * z + 1 - c)
    remote(cpart.at[1 - c], csib, 2, sibling).start()
    arrived(csib, 2)
    csum[...] = cpart[c] + csib[...]
    each(8, lambda d: remote(csum.at[z_peer(d)], crecv.at[d], 3, (dp, 2 * z_peer(d) + c)).start())
    arrived(crecv.at[pl.ds(1, 7)], 3)
    total = csum[z]
    for d in range(1, 8):
        total = total + crecv[d]
    cgath[0] = total

    each(16, lambda d: remote(cgath.at[0], cgath.at[d], 4, (d_peer(d), t)).start())
    for which in range(2):
        arecv[which, 0] = apad[which, dp]
        arrived(arecv.at[which, pl.ds(1, 15)], which)
    arrived(cgath.at[pl.ds(1, 15)], 4)

    c01 = cgath[:, 0:32, :].reshape(GROUP, 128)
    fold = cgath[:, 32:48, :].reshape(256, 128)
    other = pltpu.roll(fold, 64, 1)
    c2 = jnp.concatenate([fold.reshape(16, 16, 128), other.reshape(16, 16, 128)], axis=1).reshape(GROUP, 128)
    atok = arecv[0].reshape(GROUP, DWP)
    aog = arecv[1].reshape(GROUP, DWP)
    high, low = split(c01.T)
    left01 = dot(high, atok, NN) + dot(low, atok, NN)
    high, low = split(c2.T[0:64])
    left2 = dot(high, aog, NN) + dot(low, aog, NN)
    for half in range(2):
        cols = slice(256 * half, 256 * half + 256)
        lpart[half, 0:128, :] = left01[:, cols]
        lpart[half, 128:192, :] = left2[:, cols]

    remote(lpart.at[1 - c], lsib, 5, sibling).start()
    arrived(lsib, 5)
    lsum[...] = (lpart[c] + lsib[...]).reshape(8, 24, 256)
    each(8, lambda d: remote(lsum.at[z_peer(d)], lrecv.at[d], 6, (dp, 2 * z_peer(d) + c)).start())
    arrived(lrecv.at[pl.ds(1, 7)], 6)
    total = lsum[z]
    for d in range(1, 8):
        total = total + lrecv[d]
    lfull[c, z] = total
    each(8, lambda d: remote(lfull.at[c, z], lfull.at[c, z], 7, (dp, 2 * z_peer(d) + c)).start())
    arrived(lrecv.at[pl.ds(1, 7)], 7)
    remote(lfull.at[c], lfull.at[c], 8, sibling).start()
    arrived(lsib, 8)

    left = jnp.concatenate([lfull[0].reshape(192, 256), lfull[1].reshape(192, 256)], axis=1)
    left01 = left[0:128]
    left2 = left[128:192]
    left22 = jnp.concatenate([left2, left2], axis=0)

    high, low = split(left01)
    u01 = dot(atok, high, NT) + dot(atok, low, NT)
    high, low = split(left22)
    u22 = (dot(aog, high, NT) + dot(aog, low, NT)).reshape(16, 32, 128)
    upart[:, 0:32, :] = u01.reshape(16, 32, 128)
    lane3 = lax.broadcasted_iota(jnp.int32, (16, 16, 128), 2)
    upart[:, 32:48, :] = jnp.where(lane3 < 64, u22[:, 0:16], u22[:, 16:32])
    each(16, lambda d: remote(upart.at[d], urecv.at[d], 9, (d_back(d), t)).start())

    lane64 = lax.broadcasted_iota(jnp.int32, (64, 128), 1)
    gram01 = dot(left01, left01, NT, HIGHEST)
    gram22 = dot(left2, left22, NT, HIGHEST)
    gpart[0:4] = jnp.where(lane64 < 64, gram01[0:64], gram01[64:128]).reshape(4, 16, 128)
    gpart[4:8] = gram22.reshape(4, 16, 128)
    each(16, lambda d: remote(gpart.at[z], grecv.at[d], 10, (d_peer(d), t)).start())
    arrived(grecv.at[pl.ds(1, 15)], 10)
    total = gpart[z]
    for d in range(1, 16):
        total = total + grecv[d]
    gfull[z] = total
    each(8, lambda d: remote(gfull.at[z], gfull.at[z], 11, (dp, 2 * z_peer(d) + c)).start())
    arrived(grecv.at[pl.ds(1, 7)], 11)

    packed = gfull[...].reshape(128, 128)
    pair = pltpu.roll(packed[0:64], 64, 1)
    row64 = lax.broadcasted_iota(jnp.int32, (64, 128), 0)
    unit = jnp.where(lane64 % 64 == row64, 1.0, 0.0)
    work = [
        jnp.where(lane64 < 64, unit, pair),
        jnp.where(lane64 < 64, pair, unit),
        jnp.where(lane64 < 64, unit, packed[64:128]),
    ]
    place = (64, 0, 64)
    for j in range(63):
        top = (j // 8) * 8
        for k in range(3):
            m = work[k]
            pivot_row = m[j : j + 1, :]
            at = place[k] + j
            scaled = pivot_row * (1.0 / m[j : j + 1, at : at + 1])
            below = m[top:, :]
            column = jnp.where(row64[top:, :] > j, below[:, at : at + 1], 0.0)
            below = below - column * scaled
            work[k] = below if top == 0 else jnp.concatenate([m[:top], below], axis=0)
    inverse = []
    for k in range(3):
        m = work[k]
        diagonal = jnp.sum(jnp.where(lane64 == row64 + place[k], m, 0.0), axis=1, keepdims=True)
        m = m * lax.rsqrt(diagonal)
        inverse.append(jnp.where((lane64 < 64) == (place[k] == 64), m, 0.0))
    bd01 = jnp.concatenate([inverse[0], inverse[1]], axis=0)
    bd22 = jnp.concatenate([inverse[2], pltpu.roll(inverse[2], 64, 1)], axis=0)

    arrived(urecv.at[pl.ds(1, 15)], 9)
    total = upart[0]
    for d in range(1, 16):
        total = total + urecv[d]
    proj = jnp.concatenate(
        [dot(total[0:32], bd01, NT, HIGHEST), dot(total[32:48], bd22, NT, HIGHEST)], axis=0
    ).astype(BF16)
    pgath[c, z] = proj
    each(8, lambda d: remote(pgath.at[c, z], pgath.at[c, z], 12, (dp, 2 * z_peer(d) + c)).start())

    owner_x, owner_y = t // 4, t % 4

    @pl.when(dp == t)
    def _():
        lout[0:128, :] = dot(bd01, left01, NN, HIGHEST).astype(BF16)
        lout[128:192, :] = dot(bd22[0:64], left22, NN, HIGHEST).astype(BF16)
        each(4, lambda d: remote(lout, lout, 14, (((x + d) % 4) * 4 + y, t)).start())

    arrived(pgath.at[c, pl.ds(0, 7)], 12)
    remote(pgath.at[c], pgath.at[c], 13, sibling).start()
    arrived(pgath.at[c], 13)

    whole = jnp.concatenate([pgath[i % 2, i // 2, 0:32, :] for i in range(16)], axis=0).astype(F32)
    parts = []
    for i in range(16):
        fold = pgath[i % 2, i // 2, 32:48, :].astype(F32)
        parts += [fold, pltpu.roll(fold, 64, 1)]
    p01 = whole.T.astype(BF16)
    p2 = jnp.concatenate(parts, axis=0).T.astype(BF16)
    lhs = (p01[0:64], p01[64:128], p2[0:64])
    for j, (start, width) in enumerate(LANE_BLOCKS):
        terms = [dot(lhs[k], bmat[k, :, start : start + width], NN).astype(BF16) for k in range(3)]
        both = jnp.concatenate(terms, axis=0)
        for i in range(4):
            rpart[4 * i + j, :, 0:width] = both[48 * i : 48 * i + 48]
    each(16, lambda d: remote(rpart.at[d_peer(d)], rrecv.at[d], 16, (d_peer(d), t)).start())

    @pl.when(jnp.logical_and(y == owner_y, x != owner_x))
    def _():
        arrived(lout, 14)

    @pl.when(y == owner_y)
    def _():
        each(4, lambda d: remote(lout, lout, 15, (x * 4 + (y + d) % 4, t)).start())

    arrived(rrecv.at[pl.ds(1, 15)], 16)
    for r in range(3):
        rows = slice(16 * r, 16 * r + 16)
        total = rpart[dp, rows, :].astype(F32)
        for d in range(1, 16):
            total = total + rrecv[d, rows, :].astype(F32)
        rgath[dp, rows, :] = (total * (1.0 / 16)).astype(BF16)
    each(16, lambda d: remote(rgath.at[dp], rgath.at[dp], 17, (d_peer(d), t)).start())

    @pl.when(y != owner_y)
    def _():
        arrived(lout, 15)

    out_left[...] = lout[:, 0:DW].astype(F32)
    arrived(rrecv.at[pl.ds(1, 15)], 17)
    for i in range(4):
        for j, (start, width) in enumerate(LANE_BLOCKS):
            out_right[48 * i : 48 * i + 48, start : start + width] = rgath[4 * i + j, :, 0:width].astype(F32)

    for which in range(2):
        sent(arecv.at[which, pl.ds(1, 15)], which)
    sent(csib, 2)
    sent(crecv.at[pl.ds(1, 7)], 3)
    sent(cgath.at[pl.ds(1, 15)], 4)
    sent(lsib, 5)
    sent(lrecv.at[pl.ds(1, 7)], 6)
    sent(lrecv.at[pl.ds(1, 7)], 7)
    sent(lsib, 8)
    sent(urecv.at[pl.ds(1, 15)], 9)
    sent(grecv.at[pl.ds(1, 15)], 10)
    sent(grecv.at[pl.ds(1, 7)], 11)
    sent(pgath.at[0, pl.ds(0, 7)], 12)
    sent(pgath.at[0], 13)

    @pl.when(dp == t)
    def _():
        each(4, lambda d: sent(lout, 14))

    @pl.when(y == owner_y)
    def _():
        each(4, lambda d: sent(lout, 15))

    sent(rrecv.at[pl.ds(1, 15)], 16)
    sent(rrecv.at[pl.ds(1, 15)], 17)


def shards(tokens, out_grad, gate_pre, up_pre, hidden_grad, warm_basis):
    vmem = pltpu.VMEM
    scratch = [
        vmem((ROWS, 7424), BF16), vmem((ROWS, 7424), BF16),
        vmem((GROUP, FFW), BF16), vmem((GROUP, FFW), BF16), vmem((GROUP, FFW), BF16),
        vmem((3, 128, FFW), BF16),
        vmem((2, 16, ROWS, DWP), BF16), vmem((2, 16, ROWS, DWP), BF16),
        vmem((3, GROUP, FFW), BF16),
        vmem((2, 8, 48, 128), F32), vmem((8, 48, 128), F32), vmem((8, 48, 128), F32),
        vmem((8, 48, 128), F32), vmem((16, 48, 128), F32),
        vmem((2, 192, 256), F32), vmem((192, 256), F32), vmem((8, 24, 256), F32),
        vmem((8, 24, 256), F32), vmem((2, 8, 24, 256), F32),
        vmem((16, 48, 128), F32), vmem((16, 48, 128), F32),
        vmem((8, 16, 128), F32), vmem((16, 16, 128), F32), vmem((8, 16, 128), F32),
        vmem((48, 128), BF16), vmem((2, 8, 48, 128), BF16),
        vmem((192, DWP), BF16), vmem((192, DWP), BF16),
        vmem((16, 48, 512), BF16), vmem((16, 48, 512), BF16),
        vmem((48, 512), BF16), vmem((16, 48, 512), BF16),
        pltpu.SemaphoreType.DMA((6,)), pltpu.SemaphoreType.DMA((3, NCHUNK)),
        pltpu.SemaphoreType.DMA((18,)), pltpu.SemaphoreType.DMA((18,)),
    ]
    left, right = pl.pallas_call(
        kernel,
        out_shape=(jax.ShapeDtypeStruct((192, DW), F32), jax.ShapeDtypeStruct((192, FFW), F32)),
        in_specs=[pl.BlockSpec(memory_space=pl.ANY)] * 6,
        out_specs=(pl.BlockSpec(memory_space=pltpu.VMEM), pl.BlockSpec(memory_space=pltpu.VMEM)),
        scratch_shapes=scratch,
        compiler_params=pltpu.CompilerParams(
            collective_id=0, has_side_effects=True, vmem_limit_bytes=48 * 2**20
        ),
    )(tokens, out_grad, gate_pre, up_pre, hidden_grad, warm_basis)
    return left.reshape(3, 64, DW), right.reshape(3, 64, FFW)


def solution(mesh):
    placed = (
        P(("dp", "tensor"), None),
        P(("dp", "tensor"), None),
        P("dp", "tensor"),
        P("dp", "tensor"),
        P("dp", "tensor"),
        P(None, None, "tensor"),
    )
    return jax.shard_map(
        shards,
        mesh=mesh,
        in_specs=placed,
        out_specs=(P(None, None, "tensor"), P(None, None, "tensor")),
        check_vma=False,
    )
```

time: 532 us -> 122 us (0.23)
  waiting for transfers between devices: 426 us -> 0 us
  Pallas kernels: 0 us -> 106 us
  other arithmetic: 39.6 us -> 0 us
  matrix products: 29.6 us -> 0 us
  blocking collectives: 15.5 us -> 0 us
  between operations: 13.9 us -> 0.65 us
  local copies, waits for them, and re-layouts: 7.05 us -> 13.7 us
    psum x2 -> x0, waiting for transfers between devices: 367 us -> none  [the longest x1 271 us: shards(): left_sum = lax.psum(partial_left, ('dp', 'tensor'))]
    pallas_call x0 -> x1, Pallas kernels: none -> 106 us  [shards(): pl.pallas_call(kernel, out_shape=(jax.ShapeDtypeStruct((192, DW), F32), j...]
    reduce_scatter x1 -> x0, waiting for transfers between devices: 59.5 us -> none  [shards(): lax.psum_scatter(term.reshape(lax.axis_size('tensor') * local_rows, kinds...]
    another operation x8 -> x0, other arithmetic: 37 us -> none  [the longest x4 17.9 us: orthonormal(): lower_factor = jnp.linalg.cholesky(gram_matrix)]
    dot_general x5 -> x0, matrix products: 22.6 us -> none  [the longest x1 9.51 us: gram_of(): jnp.einsum('krd,ksd->krs', left_sum, left_sum, precision=lax.Precision.HI...]
    all_gather x1 -> x0, blocking collectives: 15.5 us -> none  [shards(): lax.all_gather(proj, 'tensor', axis=2, tiled=True)]
    unnamed x16 -> x11, local copies, waits for them, and re-layouts: 3.16 us -> 13.7 us
    another operation x1 -> x0, matrix products: 7.06 us -> none  [orthonormal(): lax.linalg.triangular_solve(lower_factor, left_sum, left_side=True, lower...]
  transfers between devices with their start and end apart: 3 -> 0, of which waited for: 3 -> 0; matrix products, arithmetic and copies ran while one was open for 0% -> 0% of each run, Pallas kernels for 0% -> 0%
where the time goes in v1:
time: 122 us; the launch traced here: 120 us
  Pallas kernels  106 us (87%)
  local copies, waits for them, and re-layouts  13.7 us (11%)
    pallas_call x1, Pallas kernels, shards(): pl.pallas_call(kernel, out_shape=(jax.ShapeDtypeStruct((192, DW), F32), j...  106 us
    unnamed x11, local copies, waits for them, and re-layouts  13.7 us

profile of v1, /device:TPU:8, one launch (start us, length us, event | category | flops | bytes accessed | tf_op | source)
XLA Modules:
  0.0 120.2 jit_solution(3607308869759159599)
XLA Ops:
  0.6 2.8 %copy.8.gate_hbm = bf16[512,1856]{1,0:T(8,128)(2,1)S(1)} copy(bf16[512,1856]{0,1:T(8,128)(2,1)} %param.8) | data formatting | bytes 3801088 | tf_op args[2]
  3.4 4.0 %copy.9.up_hbm = bf16[512,1856]{1,0:T(8,128)(2,1)} copy(bf16[512,1856]{0,1:T(8,128)(2,1)} %param.9) | data formatting | bytes 3801088 | tf_op args[3]
  7.4 0.0 copy-start
  7.4 0.0 copy-start.1
  7.4 4.0 %copy.10.hid_hbm = bf16[512,1856]{1,0:T(8,128)(2,1)} copy(bf16[512,1856]{0,1:T(8,128)(2,1)} %param.10) | data formatting | bytes 3801088 | tf_op args[4]
  11.4 0.0 copy-done
  11.4 0.0 copy-done.1
  11.4 0.0 copy-start.2
  11.4 1.0 copy-done.2
  12.4 105.9 %shard_map.77 = (f32[192,464]{1,0:T(8,128)S(1)}, f32[192,1856]{1,0:T(8,128)S(1)}) custom-call(bf16[32,7424]{1,0:T(8,128)(2,1)S(1)} %copy-done.1, bf16[32,7424]{1,0:T(8,128)(2,1)S(1)} %copy-done.2, bf16[512,1856]{1,0:T(8,128)(2,1)S(1)} %copy.8.gate_hbm, bf16[512,1856]{1,0:T(8,128)(2,1)} %copy.9.up_hbm, bf16[512,1856]{1,0:T(8,128)(2,1)} %copy.10.hid_hbm, ...), custom_call_target="tpu_custom_call" | custom-call | tf_op jit(solution)/shard_map/pallas_call | solution.py:377
  118.4 0.7 copy.13
  119.1 1.1 copy.14
Async XLA Ops:
  7.4 4.0 %copy-start = (bf16[3,64,1856]{2,1,0:T(8,128)(2,1)S(1)}, bf16[3,64,1856]{2,1,0:T(8,128)(2,1)}, u32[]{:S(2)}) copy-start(bf16[3,64,1856]{2,1,0:T(8,128)(2,1)} %warm_hbm.1) | copy-start | bytes 2138116
  7.4 4.0 %copy-start.1 = (bf16[32,7424]{1,0:T(8,128)(2,1)S(1)}, bf16[32,7424]{1,0:T(8,128)(2,1)}, u32[]{:S(2)}) copy-start(bf16[32,7424]{1,0:T(8,128)(2,1)} %tok_hbm.1) | copy-start | bytes 1425412
  11.4 1.0 copy-start.2

commit v2 on v1

--- a/solution.py
+++ b/solution.py
@@ -17,9 +17,10 @@
 DWP = 512
 FFW = 1856
 GROUP = 512
-CHUNK = 128
-NCHUNK = GROUP // CHUNK
-LANE_BLOCKS = ((0, 512), (512, 512), (1024, 512), (1536, 320))
+SPLITS = 2
+PIECE = 2048 // (4 * SPLITS)
+HALVES = tuple((4 * PIECE * h, min(4 * PIECE, FFW - 4 * PIECE * h)) for h in range(SPLITS))
+BLOCKS = ((0, 512), (512, 512), (1024, 512), (1536, 320))
 
 
 def dot(a, b, dims, precision=None):
@@ -38,12 +39,11 @@
 def kernel(
     tok_hbm, og_hbm, gate_hbm, up_hbm, hid_hbm, warm_hbm,
     out_left, out_right,
-    tok, og, gate, up, hid, wp,
+    tok, og, gate, up, hid, warm,
     apad, arecv, bmat, cpart, csib, csum, crecv, cgath,
     lpart, lsib, lsum, lrecv, lfull,
     upart, urecv, gpart, grecv, gfull,
-    pown, pgath, lown, lout,
-    rpart, rrecv, rown, rgath,
+    pgath, lout, rpart, rrecv, rgath,
     ldma, cdma, ssem, rsem,
 ):
     dp = lax.axis_index("dp")
@@ -84,16 +84,13 @@
     copies = [
         pltpu.make_async_copy(tok_hbm, tok, ldma.at[0]),
         pltpu.make_async_copy(og_hbm, og, ldma.at[1]),
-        pltpu.make_async_copy(warm_hbm.at[0], wp.at[0, pl.ds(0, 64)], ldma.at[2]),
-        pltpu.make_async_copy(warm_hbm.at[1], wp.at[1, pl.ds(64, 64)], ldma.at[3]),
-        pltpu.make_async_copy(warm_hbm.at[2], wp.at[2, pl.ds(0, 64)], ldma.at[4]),
-        pltpu.make_async_copy(warm_hbm.at[2], wp.at[2, pl.ds(64, 64)], ldma.at[5]),
+        pltpu.make_async_copy(warm_hbm, warm, ldma.at[2]),
     ]
     for copy in copies:
         copy.start()
     chunk_copies = []
-    for ch in range(NCHUNK):
-        rows = pl.ds(ch * CHUNK, CHUNK)
+    for ch, (start, width) in enumerate(BLOCKS):
+        rows = pl.ds(start, width)
         group = [
             pltpu.make_async_copy(src.at[rows], dst.at[rows], cdma.at[i, ch])
             for i, (src, dst) in enumerate(((gate_hbm, gate), (up_hbm, up), (hid_hbm, hid)))
@@ -101,8 +98,6 @@
         for copy in group:
             copy.start()
         chunk_copies.append(group)
-    wp[0, 64:128, :] = jnp.zeros((64, FFW), BF16)
-    wp[1, 0:64, :] = jnp.zeros((64, FFW), BF16)
 
     copies[0].wait()
     copies[1].wait()
@@ -120,7 +115,8 @@
         copy.wait()
 
     lane = lax.broadcasted_iota(jnp.int32, (16, 128), 1)
-    for ch in range(NCHUNK):
+    terms = [0.0, 0.0, 0.0]
+    for ch, (start, width) in enumerate(BLOCKS):
         if ch == 2:
             pl.semaphore_wait(barrier, 30)
 
@@ -133,30 +129,28 @@
             copy.wait()
 
         def swiglu(i, carry):
-            rows = pl.ds(pl.multiple_of(ch * CHUNK + i * 16, 16), 16)
-            for start, width in LANE_BLOCKS:
-                cols = pl.ds(start, width)
-                g = gate[rows, cols].astype(F32)
-                u = up[rows, cols].astype(F32)
-                h = hid[rows, cols].astype(F32)
-                s = 0.5 * jnp.tanh(0.5 * g) + 0.5
-                silu = g * s
-                slope = s * (1.0 + g * (1.0 - s))
-                bmat[0, rows, cols] = (h * u * slope).astype(BF16)
-                bmat[1, rows, cols] = (h * silu).astype(BF16)
-                bmat[2, rows, cols] = (silu * u).astype(BF16)
+            rows = pl.ds(pl.multiple_of(start + i * 16, 16), 16)
+            g = gate[rows, :].astype(F32)
+            u = up[rows, :].astype(F32)
+            h = hid[rows, :].astype(F32)
+            s = 0.5 * jnp.tanh(0.5 * g) + 0.5
+            silu = g * s
+            slope = s * (1.0 + g * (1.0 - s))
+            bmat[0, rows, :] = (h * u * slope).astype(BF16)
+            bmat[1, rows, :] = (h * silu).astype(BF16)
+            bmat[2, rows, :] = (silu * u).astype(BF16)
             return carry
 
-        lax.fori_loop(0, CHUNK // 16, swiglu, 0)
-        rows = pl.ds(ch * CHUNK, CHUNK)
-        c01 = dot(bmat[0, rows, :], wp[0], NT) + dot(bmat[1, rows, :], wp[1], NT)
-        c22 = dot(bmat[2, rows, :], wp[2], NT)
-        for i in range(CHUNK // ROWS):
-            owner = ch * (CHUNK // ROWS) + i
-            cpart[owner % 2, owner // 2, 0:32, :] = c01[32 * i : 32 * i + 32]
-            cpart[owner % 2, owner // 2, 32:48, :] = jnp.where(
-                lane < 64, c22[32 * i : 32 * i + 16], c22[32 * i + 16 : 32 * i + 32]
-            )
+        lax.fori_loop(0, width // 16, swiglu, 0, unroll=2)
+        for k in range(3):
+            terms[k] += dot(warm[k, :, start : start + width], bmat[k, start : start + width, :], NN)
+    c01 = jnp.concatenate([terms[0], terms[1]], axis=0).T
+    c22 = jnp.concatenate([terms[2], terms[2]], axis=0).T
+    for i in range(16):
+        cpart[i % 2, i // 2, 0:32, :] = c01[32 * i : 32 * i + 32]
+        cpart[i % 2, i // 2, 32:48, :] = jnp.where(
+            lane < 64, c22[32 * i : 32 * i + 16], c22[32 * i + 16 : 32 * i + 32]
+        )
 
     sibling = (dp, 2 * z + 1 - c)
     remote(cpart.at[1 - c], csib, 2, sibling).start()
@@ -209,6 +203,13 @@
     left2 = left[128:192]
     left22 = jnp.concatenate([left2, left2], axis=0)
 
+    lane64 = lax.broadcasted_iota(jnp.int32, (64, 128), 1)
+    gram01 = dot(left01, left01, NT, HIGHEST)
+    gram22 = dot(left2, left22, NT, HIGHEST)
+    gpart[0:4] = jnp.where(lane64 < 64, gram01[0:64], gram01[64:128]).reshape(4, 16, 128)
+    gpart[4:8] = gram22.reshape(4, 16, 128)
+    each(16, lambda d: remote(gpart.at[z], grecv.at[d], 10, (d_peer(d), t)).start())
+
     high, low = split(left01)
     u01 = dot(atok, high, NT) + dot(atok, low, NT)
     high, low = split(left22)
@@ -218,12 +219,6 @@
     upart[:, 32:48, :] = jnp.where(lane3 < 64, u22[:, 0:16], u22[:, 16:32])
     each(16, lambda d: remote(upart.at[d], urecv.at[d], 9, (d_back(d), t)).start())
 
-    lane64 = lax.broadcasted_iota(jnp.int32, (64, 128), 1)
-    gram01 = dot(left01, left01, NT, HIGHEST)
-    gram22 = dot(left2, left22, NT, HIGHEST)
-    gpart[0:4] = jnp.where(lane64 < 64, gram01[0:64], gram01[64:128]).reshape(4, 16, 128)
-    gpart[4:8] = gram22.reshape(4, 16, 128)
-    each(16, lambda d: remote(gpart.at[z], grecv.at[d], 10, (d_peer(d), t)).start())
     arrived(grecv.at[pl.ds(1, 15)], 10)
     total = gpart[z]
     for d in range(1, 16):
@@ -292,12 +287,15 @@
     p01 = whole.T.astype(BF16)
     p2 = jnp.concatenate(parts, axis=0).T.astype(BF16)
     lhs = (p01[0:64], p01[64:128], p2[0:64])
-    for j, (start, width) in enumerate(LANE_BLOCKS):
-        terms = [dot(lhs[k], bmat[k, :, start : start + width], NN).astype(BF16) for k in range(3)]
+    for h, (start, width) in enumerate(HALVES):
+        terms = [dot(lhs[k], bmat[k, start : start + width, :], NT).astype(BF16) for k in range(3)]
         both = jnp.concatenate(terms, axis=0)
         for i in range(4):
-            rpart[4 * i + j, :, 0:width] = both[48 * i : 48 * i + 48]
-    each(16, lambda d: remote(rpart.at[d_peer(d)], rrecv.at[d], 16, (d_peer(d), t)).start())
+            for j in range(4):
+                size = min(PIECE, width - PIECE * j)
+                if size > 0:
+                    rpart[h, 4 * i + j, :, 0:size] = both[48 * i : 48 * i + 48, PIECE * j : PIECE * j + size]
+        each(16, lambda d: remote(rpart.at[h, d_peer(d)], rrecv.at[h, d], 16 + h, (d_peer(d), t)).start())
 
     @pl.when(jnp.logical_and(y == owner_y, x != owner_x))
     def _():
@@ -307,24 +305,26 @@
     def _():
         each(4, lambda d: remote(lout, lout, 15, (x * 4 + (y + d) % 4, t)).start())
 
-    arrived(rrecv.at[pl.ds(1, 15)], 16)
-    for r in range(3):
-        rows = slice(16 * r, 16 * r + 16)
-        total = rpart[dp, rows, :].astype(F32)
-        for d in range(1, 16):
-            total = total + rrecv[d, rows, :].astype(F32)
-        rgath[dp, rows, :] = (total * (1.0 / 16)).astype(BF16)
-    each(16, lambda d: remote(rgath.at[dp], rgath.at[dp], 17, (d_peer(d), t)).start())
+    for h, (start, width) in enumerate(HALVES):
+        arrived(rrecv.at[h, pl.ds(1, 15)], 16 + h)
+        own_cols = pl.ds(pl.multiple_of(start + y * PIECE, PIECE), PIECE)
+        for r in range(3):
+            rows = slice(16 * r, 16 * r + 16)
+            total = rpart[h, dp, rows, :].astype(F32)
+            for d in range(1, 16):
+                total = total + rrecv[h, d, rows, :].astype(F32)
+            rgath[pl.ds(pl.multiple_of(x * 48 + 16 * r, 16), 16), own_cols] = (total * (1.0 / 16)).astype(BF16)
+        own = rgath.at[pl.ds(pl.multiple_of(x * 48, 16), 48), own_cols]
+        each(16, lambda d: remote(own, own, 16 + SPLITS + h, (d_peer(d), t)).start())
 
     @pl.when(y != owner_y)
     def _():
         arrived(lout, 15)
 
-    out_left[...] = lout[:, 0:DW].astype(F32)
-    arrived(rrecv.at[pl.ds(1, 15)], 17)
-    for i in range(4):
-        for j, (start, width) in enumerate(LANE_BLOCKS):
-            out_right[48 * i : 48 * i + 48, start : start + width] = rgath[4 * i + j, :, 0:width].astype(F32)
+    out_left[...] = lout[:, 0:DW]
+    for h, (start, width) in enumerate(HALVES):
+        arrived(rrecv.at[h, pl.ds(1, 15)], 16 + SPLITS + h)
+        out_right[:, start : start + width] = rgath[:, start : start + width]
 
     for which in range(2):
         sent(arecv.at[which, pl.ds(1, 15)], which)
@@ -349,42 +349,40 @@
     def _():
         each(4, lambda d: sent(lout, 15))
 
-    sent(rrecv.at[pl.ds(1, 15)], 16)
-    sent(rrecv.at[pl.ds(1, 15)], 17)
+    for h in range(2 * SPLITS):
+        sent(rrecv.at[0, pl.ds(1, 15)], 16 + h)
 
 
 def shards(tokens, out_grad, gate_pre, up_pre, hidden_grad, warm_basis):
     vmem = pltpu.VMEM
     scratch = [
         vmem((ROWS, 7424), BF16), vmem((ROWS, 7424), BF16),
-        vmem((GROUP, FFW), BF16), vmem((GROUP, FFW), BF16), vmem((GROUP, FFW), BF16),
-        vmem((3, 128, FFW), BF16),
+        vmem((FFW, GROUP), BF16), vmem((FFW, GROUP), BF16), vmem((FFW, GROUP), BF16),
+        vmem((3, 64, FFW), BF16),
         vmem((2, 16, ROWS, DWP), BF16), vmem((2, 16, ROWS, DWP), BF16),
-        vmem((3, GROUP, FFW), BF16),
+        vmem((3, FFW, GROUP), BF16),
         vmem((2, 8, 48, 128), F32), vmem((8, 48, 128), F32), vmem((8, 48, 128), F32),
         vmem((8, 48, 128), F32), vmem((16, 48, 128), F32),
         vmem((2, 192, 256), F32), vmem((192, 256), F32), vmem((8, 24, 256), F32),
         vmem((8, 24, 256), F32), vmem((2, 8, 24, 256), F32),
         vmem((16, 48, 128), F32), vmem((16, 48, 128), F32),
         vmem((8, 16, 128), F32), vmem((16, 16, 128), F32), vmem((8, 16, 128), F32),
-        vmem((48, 128), BF16), vmem((2, 8, 48, 128), BF16),
-        vmem((192, DWP), BF16), vmem((192, DWP), BF16),
-        vmem((16, 48, 512), BF16), vmem((16, 48, 512), BF16),
-        vmem((48, 512), BF16), vmem((16, 48, 512), BF16),
-        pltpu.SemaphoreType.DMA((6,)), pltpu.SemaphoreType.DMA((3, NCHUNK)),
-        pltpu.SemaphoreType.DMA((18,)), pltpu.SemaphoreType.DMA((18,)),
+        vmem((2, 8, 48, 128), BF16), vmem((192, DWP), BF16),
+        vmem((SPLITS, 16, 48, PIECE), BF16), vmem((SPLITS, 16, 48, PIECE), BF16), vmem((192, 2048), BF16),
+        pltpu.SemaphoreType.DMA((3,)), pltpu.SemaphoreType.DMA((3, 4)),
+        pltpu.SemaphoreType.DMA((16 + 2 * SPLITS,)), pltpu.SemaphoreType.DMA((16 + 2 * SPLITS,)),
     ]
     left, right = pl.pallas_call(
         kernel,
-        out_shape=(jax.ShapeDtypeStruct((192, DW), F32), jax.ShapeDtypeStruct((192, FFW), F32)),
+        out_shape=(jax.ShapeDtypeStruct((192, DW), BF16), jax.ShapeDtypeStruct((192, FFW), BF16)),
         in_specs=[pl.BlockSpec(memory_space=pl.ANY)] * 6,
         out_specs=(pl.BlockSpec(memory_space=pltpu.VMEM), pl.BlockSpec(memory_space=pltpu.VMEM)),
         scratch_shapes=scratch,
         compiler_params=pltpu.CompilerParams(
-            collective_id=0, has_side_effects=True, vmem_limit_bytes=48 * 2**20
+            collective_id=0, has_side_effects=True, vmem_limit_bytes=60 * 2**20
         ),
-    )(tokens, out_grad, gate_pre, up_pre, hidden_grad, warm_basis)
-    return left.reshape(3, 64, DW), right.reshape(3, 64, FFW)
+    )(tokens, out_grad, gate_pre.T, up_pre.T, hidden_grad.T, warm_basis)
+    return left.astype(F32).reshape(3, 64, DW), right.astype(F32).reshape(3, 64, FFW)
 
 
 def solution(mesh):

time: 122 us -> 102 us (0.84)
  local copies, waits for them, and re-layouts: 13.7 us -> 0.01 us
  Pallas kernels: 106 us -> 96.9 us
  other arithmetic: 0 us -> 3.15 us
    unnamed x11 -> x2, local copies, waits for them, and re-layouts: 13.7 us -> 0.01 us
    pallas_call x1, Pallas kernels: 106 us -> 96.9 us  [shards(): pl.pallas_call(kernel, out_shape=(jax.ShapeDtypeStruct((192, DW), BF16),...]
    reshape x0 -> x2, other arithmetic: none -> 3.15 us  [the longest x1 2.36 us: shards(): right.astype(F32).reshape(3, 64, FFW)]
where the time goes in v2:
time: 102 us; the launch traced here: 101 us
  Pallas kernels  96.9 us (95%)
  other arithmetic  3.15 us (3%)
    pallas_call x1, Pallas kernels, shards(): pl.pallas_call(kernel, out_shape=(jax.ShapeDtypeStruct((192, DW), BF16),...  96.9 us
    reshape x1, other arithmetic, shards(): right.astype(F32).reshape(3, 64, FFW)  2.36 us

profile of v2, /device:TPU:8, one launch (start us, length us, event | category | flops | bytes accessed | tf_op | source)
XLA Modules:
  0.0 100.7 jit_solution(11680466657692696294)
XLA Ops:
  0.6 96.9 %shard_map.77 = (bf16[192,464]{1,0:T(8,128)(2,1)}, bf16[192,1856]{1,0:T(8,128)(2,1)}) custom-call(bf16[32,7424]{1,0:T(8,128)(2,1)} %tok_hbm.1, bf16[32,7424]{1,0:T(8,128)(2,1)} %og_hbm.1, bf16[1856,512]{1,0:T(8,128)(2,1)} %bitcast.7, bf16[1856,512]{1,0:T(8,128)(2,1)} %bitcast.8, bf16[1856,512]{1,0:T(8,128)(2,1)} %bitcast.9, bf16[3,64,1856]{2,1,0:T(8,128)(2,1)} %warm_hbm.1), custom_call_target="tpu_custom_call" | custom-call | tf_op jit(solution)/shard_map/pallas_call | solution.py:375
  97.5 0.0 copy-start
  97.5 2.4 %convert.3 = f32[3,64,1856]{2,1,0:T(8,128)} convert(bf16[3,64,1856]{2,1,0:T(8,128)(2,1)} %bitcast.10) | non-fusion elementwise | flops 356352 | bytes 2138112 | tf_op jit(solution)/shard_map/reshape | solution.py:385
  99.9 0.0 copy-done
  99.9 0.8 convert.2
Async XLA Ops:
  97.5 2.4 %copy-start = (bf16[192,464]{1,0:T(8,128)(2,1)S(1)}, bf16[192,464]{1,0:T(8,128)(2,1)}, u32[]{:S(2)}) copy-start(bf16[192,464]{1,0:T(8,128)(2,1)} %get-tuple-element.4) | copy-start | bytes 534532

commit v3 on v2

--- a/solution.py
+++ b/solution.py
@@ -279,6 +279,14 @@
     remote(pgath.at[c], pgath.at[c], 13, sibling).start()
     arrived(pgath.at[c], 13)
 
+    @pl.when(jnp.logical_and(y == owner_y, x != owner_x))
+    def _():
+        arrived(lout, 14)
+
+    @pl.when(y == owner_y)
+    def _():
+        each(4, lambda d: remote(lout, lout, 15, (x * 4 + (y + d) % 4, t)).start())
+
     whole = jnp.concatenate([pgath[i % 2, i // 2, 0:32, :] for i in range(16)], axis=0).astype(F32)
     parts = []
     for i in range(16):
@@ -296,14 +304,6 @@
                 if size > 0:
                     rpart[h, 4 * i + j, :, 0:size] = both[48 * i : 48 * i + 48, PIECE * j : PIECE * j + size]
         each(16, lambda d: remote(rpart.at[h, d_peer(d)], rrecv.at[h, d], 16 + h, (d_peer(d), t)).start())
-
-    @pl.when(jnp.logical_and(y == owner_y, x != owner_x))
-    def _():
-        arrived(lout, 14)
-
-    @pl.when(y == owner_y)
-    def _():
-        each(4, lambda d: remote(lout, lout, 15, (x * 4 + (y + d) % 4, t)).start())
 
     for h, (start, width) in enumerate(HALVES):
         arrived(rrecv.at[h, pl.ds(1, 15)], 16 + h)

time: 102 us -> 108 us (1.059)
  Pallas kernels: 96.9 us -> 104 us
    pallas_call x1, Pallas kernels: 96.9 us -> 104 us  [shards(): pl.pallas_call(kernel, out_shape=(jax.ShapeDtypeStruct((192, DW), BF16),...]
where the time goes in v3:
time: 108 us
  Pallas kernels  104 us (96%)
  other arithmetic  3.15 us (3%)
    pallas_call x1, Pallas kernels, shards(): pl.pallas_call(kernel, out_shape=(jax.ShapeDtypeStruct((192, DW), BF16),...  104 us
    reshape x1, other arithmetic, shards(): right.astype(F32).reshape(3, 64, FFW)  2.36 us

profile of v3, /device:TPU:8, one launch (start us, length us, event | category | flops | bytes accessed | tf_op | source)
XLA Modules:
  0.0 107.6 jit_solution(15116903661170497988)
XLA Ops:
  0.6 103.8 %shard_map.77 = (bf16[192,464]{1,0:T(8,128)(2,1)}, bf16[192,1856]{1,0:T(8,128)(2,1)}) custom-call(bf16[32,7424]{1,0:T(8,128)(2,1)} %tok_hbm.1, bf16[32,7424]{1,0:T(8,128)(2,1)} %og_hbm.1, bf16[1856,512]{1,0:T(8,128)(2,1)} %bitcast.7, bf16[1856,512]{1,0:T(8,128)(2,1)} %bitcast.8, bf16[1856,512]{1,0:T(8,128)(2,1)} %bitcast.9, bf16[3,64,1856]{2,1,0:T(8,128)(2,1)} %warm_hbm.1), custom_call_target="tpu_custom_call" | custom-call | tf_op jit(solution)/shard_map/pallas_call | solution.py:375
  104.4 0.0 copy-start
  104.4 2.4 %convert.3 = f32[3,64,1856]{2,1,0:T(8,128)} convert(bf16[3,64,1856]{2,1,0:T(8,128)(2,1)} %bitcast.10) | non-fusion elementwise | flops 356352 | bytes 2138112 | tf_op jit(solution)/shard_map/reshape | solution.py:385
  106.8 0.0 copy-done
  106.8 0.8 convert.2
Async XLA Ops:
  104.4 2.4 %copy-start = (bf16[192,464]{1,0:T(8,128)(2,1)S(1)}, bf16[192,464]{1,0:T(8,128)(2,1)}, u32[]{:S(2)}) copy-start(bf16[192,464]{1,0:T(8,128)(2,1)} %get-tuple-element.4) | copy-start | bytes 534532
